TPU v7x, 128 devices: a whole 4x4x4 slice. The times are simulated.
128 devices in a mesh: dp: 8 (over y, core), fsdp: 16 (over x, z).
Axes of the slice: x: 4, y: 4, z: 4, core: 2. Of those that a mesh axis runs over, the one named last changes fastest.
Arguments:
- activations: bfloat16 [114688, 8192], P(('dp', 'fsdp')), may hold values from -6 to 6
- key_cotangent: bfloat16 [114688, 1024], P(('dp', 'fsdp')), may hold values from -0.046875 to 0.046875
- momentum: float32 [8, 8192, 1024], P('dp', 'fsdp'), may hold values from -6 to 6
- frequencies: int32 [8, 128, 16, 32], P('dp', 'fsdp'), may hold values from 0 to 4095, all different within a row
Outputs:
- update: float32 [8192, 1024], P('fsdp')
- new_momentum: float32 [8, 8192, 1024], P('dp', 'fsdp')
Inputs may be any that keep to these rules, and one draw needn't show every extreme that they name: The 32 frequencies of one tile and replica are all different.
All inputs are finite; a program needn't handle non-finite values.
Results may differ from a plain program's by a relative error of at most 0.0003.
Values may be sent and summed in bfloat16 or wider, within the bound.
No kernel may reach another device: no remote copies, remote signals or barrier semaphores. Data moves between devices by JAX's collectives and lax.ppermute only.
A program may use at most 192 MiB of HBM per device.

v0:
```python
import jax
import jax.numpy as jnp
from jax import lax
from jax.sharding import PartitionSpec as P

TILE = 64


momentum_decay = 0.999


def cosine_table(edge):
    freq_rows = jnp.arange(edge, dtype=jnp.float32)[:, None]
    positions = jnp.arange(edge, dtype=jnp.float32)[None, :]
    cosine = jnp.cos(jnp.pi * (2.0 * positions + 1.0) * freq_rows / (2.0 * edge)) * jnp.sqrt(
        2.0 / edge
    )
    scaling = jnp.where(jnp.arange(edge) == 0, jnp.sqrt(0.5), 1.0).astype(jnp.float32)
    return cosine * scaling[:, None]


def forward_tiles(matrix, cosine, edge):
    row_count, col_count = matrix.shape
    flat = matrix.reshape(row_count * (col_count // edge), edge)
    half = jnp.dot(flat, cosine.T, precision=lax.Precision.HIGHEST).reshape(
        row_count // edge, edge, col_count // edge, edge
    )
    return jnp.einsum("kn,anbl->abkl", cosine, half, precision=lax.Precision.HIGHEST)


def inverse_tiles(spectra, cosine):
    half = jnp.einsum("kn,abkl->abnl", cosine, spectra, precision=lax.Precision.HIGHEST)
    dense_part = jnp.einsum("abnl,lm->anbm", half, cosine, precision=lax.Precision.HIGHEST)
    shape_a, shape_n, shape_b, shape_m = dense_part.shape
    return dense_part.reshape(shape_a * shape_n, shape_b * shape_m)


def place_lists(values, chosen, edge):
    tiles_a, tiles_b, listed = values.shape
    index_a = jnp.arange(tiles_a, dtype=jnp.int32)[:, None, None]
    index_b = jnp.arange(tiles_b, dtype=jnp.int32)[None, :, None]
    flat = (
        jnp.zeros((tiles_a, tiles_b, edge * edge), jnp.float32)
        .at[index_a, index_b, chosen]
        .add(values)
    )
    return flat.reshape(tiles_a, tiles_b, edge, edge)


def per_device(activations, key_cotangent, momentum, frequencies):
    edge = TILE
    every_freq = lax.all_gather(frequencies, "dp", axis=0, tiled=True)
    gradient = lax.psum_scatter(
        lax.dot_general(
            activations, key_cotangent, (((0,), (0,)), ((), ())), preferred_element_type=jnp.float32
        ),
        "fsdp",
        scatter_dimension=0,
        tiled=True,
    )
    cosine = cosine_table(edge)
    moment = momentum_decay * momentum[0] + gradient
    spectra = forward_tiles(moment, cosine, edge)
    tiles_a, tiles_b = (spectra.shape[0], spectra.shape[1])
    own_freq = frequencies[0]
    values = jnp.take_along_axis(spectra.reshape(tiles_a, tiles_b, edge * edge), own_freq, axis=2)
    removed = inverse_tiles(place_lists(values, own_freq, edge), cosine)
    every_value = lax.all_gather(values[None], "dp", axis=0, tiled=True)
    replicas = every_value.shape[0]
    listed = every_value.shape[3]
    merged_values = jnp.transpose(every_value, (1, 2, 0, 3)).reshape(
        tiles_a, tiles_b, replicas * listed
    )
    merged_freq = jnp.transpose(every_freq, (1, 2, 0, 3)).reshape(
        tiles_a, tiles_b, replicas * listed
    )
    update = inverse_tiles(place_lists(merged_values, merged_freq, edge), cosine)
    return (update / replicas, (moment - removed)[None])


def solution(mesh):
    in_specs = (
        P(("dp", "fsdp"), None),
        P(("dp", "fsdp"), None),
        P("dp", "fsdp", None),
        P("dp", "fsdp", None, None),
    )
    out_specs = (P("fsdp", None), P("dp", "fsdp", None))
    return jax.shard_map(
        per_device, mesh=mesh, in_specs=in_specs, out_specs=out_specs, check_vma=False
    )
```

profile of v0, /device:TPU:1, one launch (start us, length us, event | category | flops | bytes accessed | tf_op | source)
XLA Modules:
  0.0 581.5 jit_solution(7372860981397414111)
XLA Ops:
  7.2 1.4 copy-done
  8.7 24.9 %fusion.48 = f32[8192,1024]{1,0:T(8,128)} fusion(bf16[896,8192]{1,0:T(8,128)(2,1)} %param.4, bf16[896,1024]{1,0:T(8,128)(2,1)S(1)} %copy-done), kind=kOutput, calls=%fused_computation.69 | convolution fusion | flops 15032385536 | bytes 50069504 | tf_op jit(solution)/shard_map/dot_general | solution.py:54
  33.6 0.8 copy-done.4
  34.7 0.1 and_reduce_fusion.1
  34.9 15.0 %all_gather.6 = s32[8,8,16,32]{3,2,1,0:T(8,128)S(1)} all-gather(s32[1,8,16,32]{3,2,1,0:T(8,128)S(1)} %copy-done.4), channel_id=1, replica_groups=mesh['dp'=8,'fsdp'=16] {'dp'}, dimensions={0}, use_global_device_ids=true | all-gather | bytes 147456 | tf_op jit(solution)/shard_map/all_gather | solution.py:52
  49.8 0.3 copy.27
  50.1 0.2 reshape.116
  50.5 0.1 and_reduce_fusion
  50.7 181.1 %reduce-scatter.2.cloned.1.call-done = f32[512,1024]{1,0:T(8,128)} async-done(((f32[8192,1024]{1,0:T(8,128)}), f32[512,1024]{1,0:T(8,128)}) %reduce-scatter.2.cloned.1.call-update) | async-done | bytes 2097168 | tf_op jit(solution)/shard_map/reduce_scatter | solution.py:53
  231.8 2.7 bitcast_add_fusion
  234.5 3.0 dot_general.24
  237.5 14.8 %fusion.4 = f32[8,64,16,64]{1,3,2,0:T(8,128)S(1)} fusion(f32[8,64,16,64]{3,2,1,0:T(8,128)} %dot_general.24, f32[64]{0:T(128)S(1)} %get-tuple-element.4, f32[64]{0:T(128)S(1)} %get-tuple-element.5), kind=kOutput, calls=%fused_computation.7 | convolution fusion | flops 402665472 | bytes 4194816 | tf_op jit(solution)/shard_map/dot_general | solution.py:25
  252.3 5.3 convolution_bitcast_fusion
  257.6 5.3 copy.32
  263.0 3.5 reshape.117
  266.5 40.6 %gather_fusion = f32[4096]{0:T(1024)S(1)} fusion(f32[8,16,4096]{2,1,0:T(8,128)S(1)} %reshape.117, s32[4096]{0:T(1024)S(1)} %reshape.132), kind=kCustom, calls=%fused_computation | custom fusion | bytes 81920 | tf_op jit(solution)/shard_map/jit(take_along_axis)/gather | solution.py:66
  307.4 22.4 %scatter_custom_fusion.1 = f32[524288]{0:T(1024)S(1)} fusion(s32[4096]{0:T(1024)S(1)} %reshape.144, f32[4096]{0:T(1024)S(1)} %reshape.146, f32[]{:T(128)} %constant.20.clone.1), kind=kCustom, calls=%fused_computation.14 | custom fusion | flops 4096 | bytes 2097156
  329.8 2.5 reshape.120
  332.3 8.8 %fusion.15 = f32[8,16,64,64]{3,2,1,0:T(8,128)S(1)} fusion(f32[8,16,64,64]{3,2,1,0:T(8,128)} %reshape.120, f32[64]{0:T(128)S(1)} %get-tuple-element.4, f32[64]{0:T(128)S(1)} %get-tuple-element.5), kind=kOutput, calls=%fused_computation.32 | convolution fusion | flops 402665472 | bytes 4194816 | tf_op jit(solution)/shard_map/kn,abkl->abnl/dot_general | solution.py:32
  341.1 5.5 fusion.8
  346.7 5.6 copy.41
  352.3 5.0 reshape.121
  357.3 3.3 subtract_bitcast_fusion
  360.6 14.3 %all_gather.7 = f32[8,8,16,32]{3,2,1,0:T(8,128)S(1)} all-gather(f32[1,8,16,32]{3,2,1,0:T(8,128)S(1)} %and_select_fusion.1), channel_id=1, replica_groups=mesh['dp'=8,'fsdp'=16] {'dp'}, dimensions={0}, use_global_device_ids=true | all-gather | bytes 147456 | tf_op jit(solution)/shard_map/all_gather | solution.py:68
  374.9 0.3 copy.33
  375.2 0.2 reshape.140
  375.4 171.6 %scatter_custom_fusion = f32[524288]{0:T(1024)S(1)} fusion(s32[32768]{0:T(1024)S(1)} %bitcast.73, f32[32768]{0:T(1024)S(1)} %reshape.140, f32[]{:T(128)} %constant.20.clone.1), kind=kCustom, calls=%fused_computation.16 | custom fusion | flops 32768 | bytes 2097156
  547.0 2.5 reshape.119
  549.5 8.8 %fusion.17 = f32[8,16,64,64]{3,2,1,0:T(8,128)S(1)} fusion(f32[8,16,64,64]{3,2,1,0:T(8,128)} %reshape.119, f32[64]{0:T(128)S(1)} %get-tuple-element.4, f32[64]{0:T(128)S(1)} %get-tuple-element.5), kind=kOutput, calls=%fused_computation.34 | convolution fusion | flops 402665472 | bytes 4194816 | tf_op jit(solution)/shard_map/kn,abkl->abnl/dot_general | solution.py:32
  558.3 5.5 multiply_bitcast_fusion
  563.9 5.7 copy.37
  569.6 4.8 div.31
  (33 shorter events, 0.9 us)
Async XLA Ops:
  7.2 1.5 copy-start
  7.2 224.6 %reduce-scatter.2.cloned.1.call-start = ((), (), s32[]{:S(2)}) async-start(), calls=%async_computation.1 | async-start | bytes 35651584 | tf_op jit(solution)/shard_map/reduce_scatter | solution.py:53
  33.6 0.8 copy-start.4
  33.6 1.0 copy-start.5
  33.6 1.1 copy-start.6
  234.4 3.0 copy-start.2
  352.3 5.0 copy-start.3
  563.9 10.6 %copy-start.1 = (bf16[896,1024]{1,0:T(8,128)(2,1)S(1)}, bf16[896,1024]{1,0:T(8,128)(2,1)}, u32[]{:S(2)}) copy-start(bf16[896,1024]{1,0:T(8,128)(2,1)} %param.5) | copy-start | bytes 5505028
Sparse Core Ops, SparseCore 0:
  33.7 198.0 reduce-scatter.1
where the time goes:
time: 588 us; the launch traced here: 582 us
  other arithmetic  201 us (34%)
  waiting for transfers between devices  181 us (31%)
  local copies, waits for them, and re-layouts  82.4 us (14%)
  matrix products  73.8 us (13%)
  blocking collectives  29.3 us (5%)
  between operations  14.5 us (2%)
    unnamed x8, other arithmetic  194 us
    reduce_scatter x1, waiting for transfers between devices, per_device(): lax.psum_scatter(lax.dot_general(activations, key_cotangent, (((0,), (0,)...  181 us
    gather x6, local copies, waits for them, and re-layouts, per_device(): jnp.take_along_axis(spectra.reshape(tiles_a, tiles_b, edge * edge), own_f...  40.9 us
    dot_general x1, matrix products, per_device(): lax.dot_general(activations, key_cotangent, (((0,), (0,)), ((), ())), pre...  24.9 us
    dot_general x2, matrix products, inverse_tiles(): jnp.einsum('kn,abkl->abnl', cosine, spectra, precision=lax.Precision.HIGH...  17.7 us
    all_gather x1, blocking collectives, per_device(): every_freq = lax.all_gather(frequencies, 'dp', axis=0, tiled=True)  15 us
    dot_general x1, matrix products, forward_tiles(): jnp.dot(flat, cosine.T, precision=lax.Precision.HIGHEST)  14.8 us
    all_gather x1, blocking collectives, per_device(): every_value = lax.all_gather(values[None], 'dp', axis=0, tiled=True)  14.3 us
  transfers between devices with their start and end apart: 1, of which 1 were waited for; matrix products, arithmetic and copies ran while one was open for 0% of the time, Pallas kernels for 0%

commit v1 on v0

v1 whole, which is shorter than its diff:
```python
import functools

import jax
import jax.numpy as jnp
import ml_dtypes
import numpy as np
from jax import lax
from jax.experimental import pallas as pl
from jax.experimental.pallas import tpu as pltpu
from jax.sharding import PartitionSpec as P

EDGE = 64
PICK = 32
DECAY = 0.999
RING = 4
ORDER = (2, 1, 3, 0)
GROUPS = 16
VMEM = 56 * 1024 * 1024
F32 = jnp.float32
BF16 = jnp.bfloat16


def params():
    return pltpu.CompilerParams(vmem_limit_bytes=VMEM)


def cosine_matrix():
    k = np.arange(EDGE)[:, None]
    n = np.arange(EDGE)[None, :]
    c = np.sqrt(2.0 / EDGE) * np.cos(np.pi * (2 * n + 1) * k / (2 * EDGE))
    c[0] = np.sqrt(1.0 / EDGE)
    return c


def split_table(table):
    hi = table.astype(ml_dtypes.bfloat16)
    lo = (table - hi.astype(np.float64)).astype(ml_dtypes.bfloat16)
    return np.stack([hi, lo])


def dot(a, b):
    return jnp.dot(a, b, preferred_element_type=F32)


def halves(a):
    hi = a.astype(BF16)
    return hi, (a - hi.astype(F32)).astype(BF16)


def dot_right(a, table):
    hi, lo = halves(a)
    return dot(hi, table[0]) + (dot(hi, table[1]) + dot(lo, table[0]))


def dot_left(table, a):
    hi, lo = halves(a)
    return dot(table[0], hi) + (dot(table[1], hi) + dot(table[0], lo))


def encode(value, out_ref, lanes=slice(None)):
    rows = value.shape[0]
    step = rows // GROUPS
    cube = value.reshape(GROUPS, step, value.shape[1])
    most = jnp.maximum(jnp.max(jnp.abs(cube), axis=1), 1e-30)
    power = jnp.ceil(256.0 * jnp.log2(most) + 0.5)
    inverse = 32767.0 * jnp.exp2(power * (-1.0 / 256.0))
    code = jnp.floor(cube * inverse[:, None, :] + 0.5).astype(jnp.int32).astype(jnp.int16)
    out_ref[:rows, lanes] = code.reshape(rows, value.shape[1])
    out_ref[rows:, lanes] = power.astype(jnp.int32).astype(jnp.int16)


def decode(ref, lanes=slice(None)):
    rows = ref.shape[0] - GROUPS
    step = rows // GROUPS
    scale = jnp.exp2(ref[rows:, lanes].astype(jnp.int32).astype(F32) * (1.0 / 256.0)) * (1.0 / 32767.0)
    code = ref[:rows, lanes].astype(jnp.int32).astype(F32)
    width = code.shape[1]
    return (code.reshape(GROUPS, step, width) * scale[:, None, :]).reshape(rows, width)


def matmul_kernel(modes, idx_ref, kt_ref, act_ref, *out_refs):
    product = dot(kt_ref[...], act_ref[...])
    if modes == "own":
        out_refs[0][...] = product
        return
    for half, coded in enumerate(modes):
        part = product[:, half * 128 : (half + 1) * 128]
        if coded:
            encode(part, out_refs[half])
        else:
            out_refs[half][...] = part


def matmul(kt, act, idx, modes):
    kv, tokens = kt.shape
    if modes == "own":
        shapes = [jax.ShapeDtypeStruct((kv, 1024), F32)]
        specs = [pl.BlockSpec((kv, 256), lambda i, idx: (0, i))]
    else:
        shapes = [
            jax.ShapeDtypeStruct((kv + GROUPS, 512), jnp.int16) if c else jax.ShapeDtypeStruct((kv, 512), F32)
            for c in modes
        ]
        specs = [pl.BlockSpec((s.shape[0], 128), lambda i, idx: (0, i)) for s in shapes]
    return pl.pallas_call(
        functools.partial(matmul_kernel, modes),
        out_shape=shapes,
        grid_spec=pltpu.PrefetchScalarGridSpec(
            num_scalar_prefetch=1,
            grid=(4,),
            in_specs=[
                pl.BlockSpec((kv, tokens), lambda i, idx: (0, 0)),
                pl.BlockSpec((tokens, 256), lambda i, idx: (0, idx[i])),
            ],
            out_specs=specs,
        ),
        compiler_params=params(),
        cost_estimate=pl.CostEstimate(
            flops=2 * kv * tokens * 1024, bytes_accessed=6 * 1024 * 1024, transcendentals=0
        ),
    )(idx, kt, act)


def merge_kernel(own_ref, got_ref, out_ref):
    encode(own_ref[...] + decode(got_ref), out_ref)


def merge(own, got):
    rows, cols = own.shape
    wide = pl.BlockSpec((rows + GROUPS, 128), lambda i: (0, i))
    return pl.pallas_call(
        merge_kernel,
        out_shape=jax.ShapeDtypeStruct((rows + GROUPS, cols), jnp.int16),
        grid=(cols // 128,),
        in_specs=[pl.BlockSpec((rows, 128), lambda i: (0, i)), wide],
        out_specs=wide,
        compiler_params=params(),
        cost_estimate=pl.CostEstimate(flops=8 * rows * cols, bytes_accessed=8 * rows * cols, transcendentals=0),
    )(own, got)


def combine_kernel(modes, own_ref, a0, b0, a1, b1, *out_refs):
    for half, (a, b) in enumerate(((a0, b0), (a1, b1))):
        total = own_ref[:, half * 128 : (half + 1) * 128] + (decode(a) + decode(b))
        if modes[half]:
            encode(total, out_refs[half])
        else:
            out_refs[half][...] = total


def combine(own, got, spot, modes):
    rows = own.shape[0]
    shapes = [
        jax.ShapeDtypeStruct((rows + GROUPS, 128), jnp.int16) if c else jax.ShapeDtypeStruct((rows, 128), F32)
        for c in modes
    ]
    wide = pl.BlockSpec((rows + GROUPS, 128), lambda i: (0, spot))
    return pl.pallas_call(
        functools.partial(combine_kernel, modes),
        out_shape=shapes,
        grid=(1,),
        in_specs=[pl.BlockSpec((rows, 256), lambda i: (0, spot))] + [wide] * 4,
        out_specs=[pl.BlockSpec(s.shape, lambda i: (0, 0)) for s in shapes],
        compiler_params=params(),
        cost_estimate=pl.CostEstimate(flops=rows * 2048, bytes_accessed=rows * 3072, transcendentals=0),
    )(own, *got)


def pick_rows(freq_ref, b, half):
    chosen = freq_ref[b : b + 1, half * 128 : (half + 1) * 128]
    return chosen // EDGE, chosen % EDGE


def place_matrix(high):
    tile = lax.broadcasted_iota(jnp.int32, (1, 128), 1) // PICK
    rows = lax.broadcasted_iota(jnp.int32, (256, 128), 0)
    return jnp.where(rows == high + tile * EDGE, 1.0, 0.0).astype(BF16)


def spectra_kernel(decayed_ref, right_ref, left_ref, freq_ref, *refs):
    ins, outs = refs[:18], refs[18:]
    moment_ref, spectra_ref, values_ref = outs
    sub = lax.broadcasted_iota(jnp.int32, (EDGE, 128), 0)
    for half in range(2):
        own, early, late = ins[half * 9], ins[half * 9 + 1 : half * 9 + 5], ins[half * 9 + 5 : half * 9 + 9]
        for q in range(2):
            lanes = slice(half * 256 + q * 128, half * 256 + (q + 1) * 128)
            total = own[:, q * 128 : (q + 1) * 128] + (decode(early[2 * q]) + decode(early[2 * q + 1]))
            total = total + (decode(late[2 * q]) + decode(late[2 * q + 1]))
            moment_ref[:, lanes] = decayed_ref[:, lanes] + total
        cols = slice(half * 256, (half + 1) * 256)
        half_done = dot_right(moment_ref[:, cols], right_ref)
        for block in range(4):
            rows = slice(block * 256, (block + 1) * 256)
            spectrum = dot_left(left_ref, half_done[rows])
            spectra_ref[rows, cols] = spectrum
            for inner in range(4):
                b = block * 4 + inner
                high, low = pick_rows(freq_ref, b, half)
                hi, lo = halves(spectrum[inner * EDGE : (inner + 1) * EDGE])
                place = place_matrix(high)
                picked = dot(hi, place) + dot(lo, place)
                values_ref[b : b + 1, half * 128 : (half + 1) * 128] = jnp.sum(
                    jnp.where(sub == low, picked, 0.0), axis=0, keepdims=True
                )


def spectra(decayed, right, left, freq, a, b):
    rows = decayed.shape[0]
    full = lambda s: pl.BlockSpec(s, lambda i: (0,) * len(s))
    block = lambda r, c, j: pl.BlockSpec((r, c), lambda i: (0, j))
    specs = [full(decayed.shape), full(right.shape), full(left.shape), full(freq.shape)]
    operands = [decayed, right, left, freq]
    for own, early, late in (a, b):
        operands += [own, *early, *late]
        specs += [block(rows, 256, 3)] + [block(rows + GROUPS, 128, 3)] * 4 + [block(rows + GROUPS, 128, 0)] * 4
    shapes = [
        jax.ShapeDtypeStruct((rows, 512), F32),
        jax.ShapeDtypeStruct((rows, 512), F32),
        jax.ShapeDtypeStruct((16, 256), F32),
    ]
    return pl.pallas_call(
        spectra_kernel,
        out_shape=shapes,
        grid=(1,),
        in_specs=specs,
        out_specs=[full(s.shape) for s in shapes],
        compiler_params=params(),
        cost_estimate=pl.CostEstimate(flops=10**9, bytes_accessed=16 * 1024 * 1024, transcendentals=0),
    )(*operands)


def remove_kernel(moment_ref, spectra_ref, left_ref, right_ref, freq_ref, out_ref):
    sub = lax.broadcasted_iota(jnp.int32, (EDGE, 128), 0)
    for half in range(2):
        cols = slice(half * 256, (half + 1) * 256)
        for block in range(4):
            rows = slice(block * 256, (block + 1) * 256)
            masks = []
            for inner in range(4):
                high, low = pick_rows(freq_ref, block * 4 + inner, half)
                at_low = jnp.where(sub == low, 1.0, 0.0).astype(BF16)
                masks.append(
                    lax.dot_general(
                        at_low, place_matrix(high), (((1,), (1,)), ((), ())), preferred_element_type=F32
                    )
                )
            kept = spectra_ref[rows, cols] * jnp.concatenate(masks, axis=0)
            removed = dot_right(dot_left(left_ref, kept), right_ref)
            out_ref[0, cols, rows] = (moment_ref[rows, cols] - removed).T


def remove(moment, spectrum, left, right, freq):
    rows, cols = moment.shape
    return pl.pallas_call(
        remove_kernel,
        out_shape=jax.ShapeDtypeStruct((1, cols, rows), F32),
        compiler_params=params(),
        cost_estimate=pl.CostEstimate(flops=10**9, bytes_accessed=6 * 1024 * 1024, transcendentals=0),
    )(moment, spectrum, left, right, freq)


def update_kernel(left_ref, right_ref, *refs):
    lists, (out_ref, values, chosen) = refs[:8], refs[8:]
    step = pl.program_id(0)

    @pl.when(step == 0)
    def _():
        for a in range(8):
            cut = slice(a * PICK, (a + 1) * PICK)
            values[a] = jnp.concatenate([r[:16, cut] for r in lists], axis=1)
            chosen[a] = jnp.concatenate([r[16:, cut] for r in lists], axis=1).astype(jnp.int32)

    sub = lax.broadcasted_iota(jnp.int32, (EDGE, 256), 0)
    for group in range(4):
        strips = []
        for inner_a in range(4):
            a = step * 4 + inner_a
            tiles = []
            for inner_b in range(4):
                b = group * 4 + inner_b
                value = values[a, b : b + 1, :]
                where = chosen[a, b : b + 1, :]
                hi, lo = halves(value)
                hit = sub == where // EDGE
                zero = jnp.zeros((EDGE, 256), F32)
                lhs = jnp.concatenate(
                    [
                        jnp.where(hit, hi.astype(F32), zero).astype(BF16),
                        jnp.where(hit, lo.astype(F32), zero).astype(BF16),
                    ],
                    axis=0,
                )
                rhs = jnp.where(sub == where % EDGE, 1.0, 0.0).astype(BF16)
                both = lax.dot_general(lhs, rhs, (((1,), (1,)), ((), ())), preferred_element_type=F32)
                tiles.append(both[:EDGE] + both[EDGE:])
            strips.append(jnp.concatenate(tiles, axis=1))
        spectrum = jnp.concatenate(strips, axis=0)
        out_ref[:, group * 256 : (group + 1) * 256] = dot_right(dot_left(left_ref, spectrum), right_ref) * 0.125


def update_of(lists, left, right):
    full = lambda s: pl.BlockSpec(s, lambda i: (0,) * len(s))
    return pl.pallas_call(
        update_kernel,
        out_shape=jax.ShapeDtypeStruct((512, 1024), F32),
        grid=(2,),
        in_specs=[full(left.shape), full(right.shape)] + [full((32, 256))] * 8,
        out_specs=pl.BlockSpec((256, 1024), lambda i: (i, 0)),
        scratch_shapes=[pltpu.VMEM((8, 16, 256), F32), pltpu.VMEM((8, 16, 256), jnp.int32)],
        compiler_params=params(),
        cost_estimate=pl.CostEstimate(flops=2 * 10**9, bytes_accessed=3 * 1024 * 1024, transcendentals=0),
    )(left, right, *lists)


def shift(value, axis, by):
    if axis == "x":
        pairs = [(x * 4 + z, (x + by) % 4 * 4 + z) for x in range(4) for z in range(4)]
    else:
        pairs = [(x * 4 + z, x * 4 + (z + by) % 4) for x in range(4) for z in range(4)]
    return lax.ppermute(value, "fsdp", pairs)


def first_stage(kt, act, axis, here, there):
    other = "z" if axis == "x" else "x"

    def blocks(away):
        along = (here + away) % RING
        ids = []
        for turn in ORDER:
            across = (there + turn) % RING
            ids.append(2 * (4 * along + across) if axis == "x" else 2 * (4 * across + along) + 1)
        return jnp.stack(ids).astype(jnp.int32)

    far_up, far_down = matmul(kt, act, blocks(2), (True, True))
    got_up, got_down = shift(far_up, axis, 1), shift(far_down, axis, -1)
    keep_up, alone_up = matmul(kt, act, blocks(1), (False, True))
    alone_down, keep_down = matmul(kt, act, blocks(3), (True, False))
    single_up, single_down = shift(alone_up, axis, 1), shift(alone_down, axis, -1)
    (own,) = matmul(kt, act, blocks(0), "own")
    double_up = shift(merge(keep_up, got_up), axis, 1)
    double_down = shift(merge(keep_down, got_down), axis, -1)
    return other, own, (double_up, single_down, single_up, double_down)


def second_stage(other, own, early):
    far_up, far_down = combine(own, early, 0, (True, True))
    got_up, got_down = shift(far_up, other, 1), shift(far_down, other, -1)
    keep_up, alone_up = combine(own, early, 1, (False, True))
    alone_down, keep_down = combine(own, early, 2, (True, False))
    single_up, single_down = shift(alone_up, other, 1), shift(alone_down, other, -1)
    double_up = shift(merge(keep_up, got_up), other, 1)
    double_down = shift(merge(keep_down, got_down), other, -1)
    return own, early, (double_up, single_down, single_up, double_down)


def exchange(mine):
    partner = lax.ppermute(mine, "dp", [(i, i ^ 1) for i in range(8)])
    out = [mine, partner]
    pair = jnp.concatenate([mine, partner], axis=0)
    for by in (1, 2, 3):
        got = lax.ppermute(pair, "dp", [(y * 2 + c, (y + by) % 4 * 2 + c) for y in range(4) for c in range(2)])
        out += [got[:32], got[32:]]
    return out


def per_device(activations, key_cotangent, momentum, frequencies):
    place = lax.axis_index("fsdp")
    x, z = place // RING, place % RING
    kt = key_cotangent.T
    cosine = cosine_matrix()
    by_c = jnp.asarray(split_table(np.kron(np.eye(4), cosine)))
    by_ct = jnp.asarray(split_table(np.kron(np.eye(4), cosine.T)))
    decayed = (DECAY * momentum[0]).T
    freq = jnp.transpose(frequencies[0], (1, 0, 2)).reshape(16, 256)
    first_a = first_stage(kt, activations, "x", x, z)
    first_b = first_stage(kt, activations, "z", z, x)
    second_a = second_stage(*first_a)
    second_b = second_stage(*first_b)
    moment, spectrum, values = spectra(decayed, by_ct, by_c, freq, second_a, second_b)
    lists = exchange(jnp.concatenate([values, freq.astype(F32)], axis=0))
    new_momentum = remove(moment, spectrum, by_ct, by_c, freq)
    update = update_of(lists, by_ct, by_c)
    return update, new_momentum


def solution(mesh):
    in_specs = (
        P(("dp", "fsdp"), None),
        P(("dp", "fsdp"), None),
        P("dp", "fsdp", None),
        P("dp", "fsdp", None, None),
    )
    out_specs = (P("fsdp", None), P("dp", "fsdp", None))
    return jax.shard_map(per_device, mesh=mesh, in_specs=in_specs, out_specs=out_specs, check_vma=False)
```

time: 588 us -> 220 us (0.37)
  other arithmetic: 201 us -> 8.14 us
  waiting for transfers between devices: 181 us -> 28.7 us
  Pallas kernels: 0 us -> 128 us
  matrix products: 73.8 us -> 0 us
  local copies, waits for them, and re-layouts: 82.4 us -> 9.41 us
  starting transfers between devices: 0.04 us -> 43 us
  blocking collectives: 29.3 us -> 0 us
  between operations: 14.5 us -> 1.02 us
    unnamed x8 -> x0, other arithmetic: 194 us -> none
    reduce_scatter x1 -> x0, waiting for transfers between devices: 181 us -> none  [per_device(): lax.psum_scatter(lax.dot_general(activations, key_cotangent, (((0,), (0,)...]
    pallas_call x0 -> x25, Pallas kernels: none -> 128 us  [the longest x8 55.4 us: matmul(): pl.pallas_call(functools.partial(matmul_kernel, modes), out_shape=shapes,...]
    dot_general x7 -> x0, matrix products: 73.8 us -> none  [the longest x1 24.9 us: per_device(): lax.dot_general(activations, key_cotangent, (((0,), (0,)), ((), ())), pre...]
    ppermute x0 -> x28, starting transfers between devices: none -> 43 us  [the longest x24 30.4 us: shift(): return lax.ppermute(value, 'fsdp', pairs)]
    gather x6 -> x0, local copies, waits for them, and re-layouts: 40.9 us -> none  [per_device(): jnp.take_along_axis(spectra.reshape(tiles_a, tiles_b, edge * edge), own_f...]
    all_gather x2 -> x0, blocking collectives: 29.3 us -> none  [the longest x1 15 us: per_device(): every_freq = lax.all_gather(frequencies, 'dp', axis=0, tiled=True)]
    ppermute x0 -> x28, waiting for transfers between devices: none -> 28.7 us  [the longest x24 23.8 us: shift(): return lax.ppermute(value, 'fsdp', pairs)]
  transfers between devices with their start and end apart: 1 -> 28, of which waited for: 1 -> 7; matrix products, arithmetic and copies ran while one was open for 0% -> 4% of each run, Pallas kernels for 0% -> 46%
where the time goes in v1:
time: 220 us; the launch traced here: 218 us
  Pallas kernels  128 us (58%)
  starting transfers between devices  43 us (20%)
  waiting for transfers between devices  28.7 us (13%)
  local copies, waits for them, and re-layouts  9.41 us (4%)
  other arithmetic  8.14 us (4%)
    pallas_call x8, Pallas kernels, matmul(): pl.pallas_call(functools.partial(matmul_kernel, modes), out_shape=shapes,...  55.4 us
    ppermute x24, starting transfers between devices, shift(): return lax.ppermute(value, 'fsdp', pairs)  30.4 us
    pallas_call x8, Pallas kernels, merge(): pl.pallas_call(merge_kernel, out_shape=jax.ShapeDtypeStruct((rows + GROUP...  25.3 us
    ppermute x24, waiting for transfers between devices, shift(): return lax.ppermute(value, 'fsdp', pairs)  23.8 us
    pallas_call x6, Pallas kernels, combine(): pl.pallas_call(functools.partial(combine_kernel, modes), out_shape=shapes...  17.6 us
    pallas_call x1, Pallas kernels, spectra(): pl.pallas_call(spectra_kernel, out_shape=shapes, grid=(1,), in_specs=spec...  10.6 us
    pallas_call x1, Pallas kernels, update_of(): pl.pallas_call(update_kernel, out_shape=jax.ShapeDtypeStruct((512, 1024),...  10.4 us
    pallas_call x1, Pallas kernels, remove(): pl.pallas_call(remove_kernel, out_shape=jax.ShapeDtypeStruct((1, cols, ro...  8.96 us
  transfers between devices with their start and end apart: 28, of which 7 were waited for; matrix products, arithmetic and copies ran while one was open for 4% of the time, Pallas kernels for 46%

profile of v1, /device:TPU:1, one launch (start us, length us, event | category | flops | bytes accessed | tf_op | source)
XLA Modules:
  0.0 218.4 jit_solution(3720934359041875282)
XLA Ops:
  0.7 3.8 %copy.10 = bf16[896,1024]{0,1:T(8,128)(2,1)} copy(bf16[896,1024]{1,0:T(8,128)(2,1)} %param.7) | data formatting | bytes 3670016 | tf_op args[1]
  5.1 7.1 %shard_map.90 = (s16[1040,512]{1,0:T(8,128)(2,1)}, s16[1040,512]{1,0:T(8,128)(2,1)}) custom-call(s32[4]{0:T(128)} %pad_add_fusion.6.idx_ref, bf16[1024,896]{1,0:T(8,128)(2,1)} %bitcast.40, bf16[896,8192]{1,0:T(8,128)(2,1)} %act_ref.15), custom_call_target="tpu_custom_call" | custom-call | flops 1879048192 | bytes 6291456 | tf_op jit(solution)/shard_map/pallas_call | solution.py:105
  17.5 7.1 %shard_map.79 = (s16[1040,512]{1,0:T(8,128)(2,1)}, s16[1040,512]{1,0:T(8,128)(2,1)}) custom-call(s32[4]{0:T(128)} %pad_add_fusion.2.idx_ref, bf16[1024,896]{1,0:T(8,128)(2,1)} %bitcast.41, bf16[896,8192]{1,0:T(8,128)(2,1)} %act_ref.15), custom_call_target="tpu_custom_call" | custom-call | flops 1879048192 | bytes 6291456 | tf_op jit(solution)/shard_map/pallas_call | solution.py:105
  27.7 6.8 %shard_map.92 = (s16[1040,512]{1,0:T(8,128)(2,1)}, f32[1024,512]{1,0:T(8,128)}) custom-call(s32[4]{0:T(128)} %pad_add_fusion.7.idx_ref, bf16[1024,896]{1,0:T(8,128)(2,1)} %bitcast.42, bf16[896,8192]{1,0:T(8,128)(2,1)} %act_ref.15), custom_call_target="tpu_custom_call" | custom-call | flops 1879048192 | bytes 6291456 | tf_op jit(solution)/shard_map/pallas_call | solution.py:105
  36.7 6.8 %shard_map.89 = (f32[1024,512]{1,0:T(8,128)}, s16[1040,512]{1,0:T(8,128)(2,1)}) custom-call(s32[4]{0:T(128)} %pad_add_fusion.5.idx_ref, bf16[1024,896]{1,0:T(8,128)(2,1)} %bitcast.43, bf16[896,8192]{1,0:T(8,128)(2,1)} %act_ref.15), custom_call_target="tpu_custom_call" | custom-call | flops 1879048192 | bytes 6291456 | tf_op jit(solution)/shard_map/pallas_call | solution.py:105
  44.5 4.2 %shard_map.91 = s16[1040,512]{1,0:T(8,128)(2,1)} custom-call(f32[1024,512]{1,0:T(8,128)} %get-tuple-element.41.own_ref, s16[1040,512]{1,0:T(8,128)(2,1)} %copy-done.3), custom_call_target="tpu_custom_call" | custom-call | flops 4194304 | bytes 4194304 | tf_op jit(solution)/shard_map/pallas_call | solution.py:131
  49.3 6.8 %shard_map.81 = (s16[1040,512]{1,0:T(8,128)(2,1)}, f32[1024,512]{1,0:T(8,128)}) custom-call(s32[4]{0:T(128)} %pad_add_fusion.3.idx_ref, bf16[1024,896]{1,0:T(8,128)(2,1)} %bitcast.44, bf16[896,8192]{1,0:T(8,128)(2,1)} %act_ref.15), custom_call_target="tpu_custom_call" | custom-call | flops 1879048192 | bytes 6291456 | tf_op jit(solution)/shard_map/pallas_call | solution.py:105
  56.1 4.3 %shard_map.93 = s16[1040,512]{1,0:T(8,128)(2,1)} custom-call(f32[1024,512]{1,0:T(8,128)} %get-tuple-element.45.own_ref, s16[1040,512]{1,0:T(8,128)(2,1)} %collective-permute-done.16.got_ref), custom_call_target="tpu_custom_call" | custom-call | flops 4194304 | bytes 4194304 | tf_op jit(solution)/shard_map/pallas_call | solution.py:131
  60.4 2.7 %collective-permute-start.2 = (s16[1040,512]{1,0:T(8,128)(2,1)}, s16[1040,512]{1,0:T(8,128)(2,1)}, u32[]{:S(2)}, u32[]{:S(2)}) collective-permute-start(s16[1040,512]{1,0:T(8,128)(2,1)} %get-tuple-element.31), channel_id=1, source_target_pairs={{0,12},{1,13},{2,14},{3,15},{4,0},{5,1},{6,2},{7,3},{8,4},{9,5},{1... | collective-permute-start | bytes 3194888 | tf_op jit(solution)/shard_map/ppermute | solution.py:321
  63.0 2.7 %collective-permute-start.17 = (s16[1040,512]{1,0:T(8,128)(2,1)}, s16[1040,512]{1,0:T(8,128)(2,1)}, u32[]{:S(2)}, u32[]{:S(2)}) collective-permute-start(s16[1040,512]{1,0:T(8,128)(2,1)} %shard_map.93), channel_id=1, source_target_pairs={{0,3},{1,0},{2,1},{3,2},{4,7},{5,4},{6,5},{7,6},{8,11},{9,8},{10,9... | collective-permute-start | bytes 3194888 | tf_op jit(solution)/shard_map/ppermute | solution.py:321
  66.4 6.8 %shard_map.78 = (f32[1024,512]{1,0:T(8,128)}, s16[1040,512]{1,0:T(8,128)(2,1)}) custom-call(s32[4]{0:T(128)} %pad_add_fusion.1.idx_ref, bf16[1024,896]{1,0:T(8,128)(2,1)} %bitcast.45, bf16[896,8192]{1,0:T(8,128)(2,1)} %act_ref.15), custom_call_target="tpu_custom_call" | custom-call | flops 1879048192 | bytes 6291456 | tf_op jit(solution)/shard_map/pallas_call | solution.py:105
  73.2 4.2 %shard_map.82 = s16[1040,512]{1,0:T(8,128)(2,1)} custom-call(f32[1024,512]{1,0:T(8,128)} %get-tuple-element.33.own_ref, s16[1040,512]{1,0:T(8,128)(2,1)} %collective-permute-done.4.got_ref), custom_call_target="tpu_custom_call" | custom-call | flops 4194304 | bytes 4194304 | tf_op jit(solution)/shard_map/pallas_call | solution.py:131
  77.4 4.2 %shard_map.80 = s16[1040,512]{1,0:T(8,128)(2,1)} custom-call(f32[1024,512]{1,0:T(8,128)} %get-tuple-element.29.own_ref, s16[1040,512]{1,0:T(8,128)(2,1)} %collective-permute-done.got_ref), custom_call_target="tpu_custom_call" | custom-call | flops 4194304 | bytes 4194304 | tf_op jit(solution)/shard_map/pallas_call | solution.py:131
  84.4 6.7 %collective-permute-done.13.a0.refs_10_ = s16[1040,512]{1,0:T(8,128)(2,1)S(1)} collective-permute-done((s16[1040,512]{1,0:T(8,128)(2,1)}, s16[1040,512]{1,0:T(8,128)(2,1)S(1)}, u32[]{:S(2)}, u32[]{:S(2)}) %collective-permute-start.13) | collective-permute-done | bytes 1064992 | tf_op jit(solution)/shard_map/ppermute | solution.py:321
  91.8 6.9 %shard_map.88.own_ref.refs_9_ = f32[1024,1024]{1,0:T(8,128)} custom-call(s32[4]{0:T(128)} %pad_add_fusion.4.idx_ref, bf16[1024,896]{1,0:T(8,128)(2,1)} %bitcast.46, bf16[896,8192]{1,0:T(8,128)(2,1)} %act_ref.15), custom_call_target="tpu_custom_call" | custom-call | flops 1879048192 | bytes 6291456 | tf_op jit(solution)/shard_map/pallas_call | solution.py:105
  98.8 2.9 %shard_map.95 = (s16[1040,128]{1,0:T(8,128)(2,1)}, s16[1040,128]{1,0:T(8,128)(2,1)}) custom-call(f32[1024,1024]{1,0:T(8,128)} %shard_map.88.own_ref.refs_9_, s16[1040,512]{1,0:T(8,128)(2,1)} %copy-done.2, s16[1040,512]{1,0:T(8,128)(2,1)} %copy-done, s16[1040,512]{1,0:T(8,128)(2,1)} %copy-done.1, s16[1040,512]{1,0:T(8,128)(2,1)} %collective-permute-done.17.b1.refs_13_), custom_call_target="tpu_custom_call" | custom-call | flops 2097152 | bytes 3145728 | tf_op jit(solution)/shard_map/pallas_call | solution.py:158
  104.9 6.9 %shard_map.77.own_ref.refs_0_ = f32[1024,1024]{1,0:T(8,128)} custom-call(s32[4]{0:T(128)} %pad_add_fusion.idx_ref, bf16[1024,896]{1,0:T(8,128)(2,1)} %bitcast.47, bf16[896,8192]{1,0:T(8,128)(2,1)} %act_ref.15), custom_call_target="tpu_custom_call" | custom-call | flops 1879048192 | bytes 6291456 | tf_op jit(solution)/shard_map/pallas_call | solution.py:105
  111.9 3.0 %shard_map.97 = (s16[1040,128]{1,0:T(8,128)(2,1)}, f32[1024,128]{1,0:T(8,128)}) custom-call(f32[1024,1024]{1,0:T(8,128)} %shard_map.88.own_ref.refs_9_, s16[1040,512]{1,0:T(8,128)(2,1)} %copy-done.2, s16[1040,512]{1,0:T(8,128)(2,1)} %copy-done, s16[1040,512]{1,0:T(8,128)(2,1)} %copy-done.1, s16[1040,512]{1,0:T(8,128)(2,1)} %collective-permute-done.17.b1.refs_13_), custom_call_target="tpu_custom_call" | custom-call | flops 2097152 | bytes 3145728 | tf_op jit(solution)/shard_map/pallas_call | solution.py:158
  114.8 2.7 %collective-permute-start.20 = (s16[1040,128]{1,0:T(8,128)(2,1)}, s16[1040,128]{1,0:T(8,128)(2,1)S(1)}, u32[]{:S(2)}, u32[]{:S(2)}) collective-permute-start(s16[1040,128]{1,0:T(8,128)(2,1)} %get-tuple-element.49), channel_id=1, source_target_pairs={{0,12},{1,13},{2,14},{3,15},{4,0},{5,1},{6,2},{7,3},{8,4},{9,5},{1... | collective-permute-start | bytes 798728 | tf_op jit(solution)/shard_map/ppermute | solution.py:321
  117.5 10.6 %collective-permute-done.1.a0.refs_1_ = s16[1040,512]{1,0:T(8,128)(2,1)} collective-permute-done((s16[1040,512]{1,0:T(8,128)(2,1)}, s16[1040,512]{1,0:T(8,128)(2,1)}, u32[]{:S(2)}, u32[]{:S(2)}) %collective-permute-start.1) | collective-permute-done | bytes 1064992 | tf_op jit(solution)/shard_map/ppermute | solution.py:321
  128.1 2.9 %shard_map.84 = (s16[1040,128]{1,0:T(8,128)(2,1)}, s16[1040,128]{1,0:T(8,128)(2,1)}) custom-call(f32[1024,1024]{1,0:T(8,128)} %shard_map.77.own_ref.refs_0_, s16[1040,512]{1,0:T(8,128)(2,1)} %collective-permute-done.1.a0.refs_1_, s16[1040,512]{1,0:T(8,128)(2,1)} %collective-permute-done.2.b0.refs_2_, s16[1040,512]{1,0:T(8,128)(2,1)} %collective-permute-done.3.a1.refs_3_, ...), custom_call_target="tpu_custom_call" | custom-call | flops 2097152 | bytes 3145728 | tf_op jit(solution)/shard_map/pallas_call | solution.py:158
  132.5 2.9 %shard_map.94 = (f32[1024,128]{1,0:T(8,128)}, s16[1040,128]{1,0:T(8,128)(2,1)}) custom-call(f32[1024,1024]{1,0:T(8,128)} %shard_map.88.own_ref.refs_9_, s16[1040,512]{1,0:T(8,128)(2,1)} %copy-done.2, s16[1040,512]{1,0:T(8,128)(2,1)} %copy-done, s16[1040,512]{1,0:T(8,128)(2,1)} %copy-done.1, s16[1040,512]{1,0:T(8,128)(2,1)} %collective-permute-done.17.b1.refs_13_), custom_call_target="tpu_custom_call" | custom-call | flops 2097152 | bytes 3145728 | tf_op jit(solution)/shard_map/pallas_call | solution.py:158
  135.4 3.0 %shard_map.86 = (s16[1040,128]{1,0:T(8,128)(2,1)}, f32[1024,128]{1,0:T(8,128)}) custom-call(f32[1024,1024]{1,0:T(8,128)} %shard_map.77.own_ref.refs_0_, s16[1040,512]{1,0:T(8,128)(2,1)} %collective-permute-done.1.a0.refs_1_, s16[1040,512]{1,0:T(8,128)(2,1)} %collective-permute-done.2.b0.refs_2_, s16[1040,512]{1,0:T(8,128)(2,1)} %collective-permute-done.3.a1.refs_3_, ...), custom_call_target="tpu_custom_call" | custom-call | flops 2097152 | bytes 3145728 | tf_op jit(solution)/shard_map/pallas_call | solution.py:158
  142.1 2.9 %shard_map.83 = (f32[1024,128]{1,0:T(8,128)}, s16[1040,128]{1,0:T(8,128)(2,1)}) custom-call(f32[1024,1024]{1,0:T(8,128)} %shard_map.77.own_ref.refs_0_, s16[1040,512]{1,0:T(8,128)(2,1)} %collective-permute-done.1.a0.refs_1_, s16[1040,512]{1,0:T(8,128)(2,1)} %collective-permute-done.2.b0.refs_2_, s16[1040,512]{1,0:T(8,128)(2,1)} %collective-permute-done.3.a1.refs_3_, ...), custom_call_target="tpu_custom_call" | custom-call | flops 2097152 | bytes 3145728 | tf_op jit(solution)/shard_map/pallas_call | solution.py:158
  156.2 2.7 %collective-permute-start.11 = (s16[1040,128]{1,0:T(8,128)(2,1)}, s16[1040,128]{1,0:T(8,128)(2,1)S(1)}, u32[]{:S(2)}, u32[]{:S(2)}) collective-permute-start(s16[1040,128]{1,0:T(8,128)(2,1)} %shard_map.87), channel_id=1, source_target_pairs={{0,3},{1,0},{2,1},{3,2},{4,7},{5,4},{6,5},{7,6},{8,11},{9,8},{10,9... | collective-permute-start | bytes 798728 | tf_op jit(solution)/shard_map/ppermute | solution.py:321
  162.9 4.0 %collective-permute-done.7.refs_5_ = s16[1040,128]{1,0:T(8,128)(2,1)S(1)} collective-permute-done((s16[1040,128]{1,0:T(8,128)(2,1)}, s16[1040,128]{1,0:T(8,128)(2,1)S(1)}, u32[]{:S(2)}, u32[]{:S(2)}) %collective-permute-start.7) | collective-permute-done | bytes 266272 | tf_op jit(solution)/shard_map/ppermute | solution.py:321
  167.6 10.6 %shard_map.99 = (f32[1024,512]{1,0:T(8,128)}, f32[1024,512]{1,0:T(8,128)}, f32[16,256]{1,0:T(8,128)}) custom-call(f32[1024,512]{1,0:T(8,128)} %multiply_bitcast_fusion.decayed_ref, bf16[2,256,256]{2,1,0:T(8,128)(2,1)} %constant.136.clone.right_ref.left_ref, bf16[2,256,256]{2,1,0:T(8,128)(2,1)} %constant.135.clone.left_ref.right_ref, s32[16,256]{1,0:T(8,128)} %copy-done.16, ...), custom_call_target="tpu_custom_call" | custom-call | flops 1000000000 | bytes 16777216 | tf_op jit(solution)/shard_map/pallas_call | solution.py:222
  178.9 8.8 %collective-permute-start.24 = (f32[32,256]{1,0:T(8,128)S(1)}, f32[32,256]{1,0:T(8,128)S(1)}, u32[]{:S(2)}, u32[]{:S(2)}) collective-permute-start(f32[32,256]{1,0:T(8,128)S(1)} %pad_maximum_fusion.1.refs_0_), channel_id=1, source_target_pairs={{0,16},{16,0},{32,48},{48,32},{64,80},{80,64},{96,112},{112,96},{1... | collective-permute-start | bytes 98312 | tf_op jit(solution)/shard_map/ppermute | solution.py:358
  189.3 2.7 %collective-permute-start.27 = (f32[64,256]{1,0:T(8,128)S(1)}, f32[64,256]{1,0:T(8,128)S(1)}, u32[]{:S(2)}, u32[]{:S(2)}) collective-permute-start(f32[64,256]{1,0:T(8,128)S(1)} %pad_maximum_fusion), channel_id=1, source_target_pairs={{0,96},{16,112},{32,0},{48,16},{64,32},{80,48},{96,64},{112,80},{1... | collective-permute-start | bytes 196616 | tf_op jit(solution)/shard_map/ppermute | solution.py:362
  192.0 9.0 %shard_map.101 = f32[1,512,1024]{2,1,0:T(8,128)} custom-call(f32[1024,512]{1,0:T(8,128)} %get-tuple-element.54.moment_ref, f32[1024,512]{1,0:T(8,128)} %get-tuple-element.55.spectra_ref, bf16[2,256,256]{2,1,0:T(8,128)(2,1)} %constant.136.clone.right_ref.left_ref, bf16[2,256,256]{2,1,0:T(8,128)(2,1)} %constant.135.clone.left_ref.right_ref, s32[16,256]{1,0:T(8,128)} %copy-done.16), custom_call_target="tpu_custom_call" | custom-call | flops 1000000000 | bytes 6291456 | tf_op jit(solution)/shard_map/pallas_call | solution.py:255
  202.7 3.0 %collective-permute-done.26 = f32[64,256]{1,0:T(8,128)S(1)} collective-permute-done((f32[64,256]{1,0:T(8,128)S(1)}, f32[64,256]{1,0:T(8,128)S(1)}, u32[]{:S(2)}, u32[]{:S(2)}) %collective-permute-start.26) | collective-permute-done | bytes 65568 | tf_op jit(solution)/shard_map/ppermute | solution.py:362
  208.0 10.4 %shard_map.100 = f32[512,1024]{1,0:T(8,128)} custom-call(bf16[2,256,256]{2,1,0:T(8,128)(2,1)} %constant.136.clone.right_ref.left_ref, bf16[2,256,256]{2,1,0:T(8,128)(2,1)} %constant.135.clone.left_ref.right_ref, f32[32,256]{1,0:T(8,128)} %copy-done.18, f32[32,256]{1,0:T(8,128)} %copy-done.19, f32[32,256]{1,0:T(8,128)} %get-tuple-element.61.refs_2_, ...), custom_call_target="tpu_custom_call" | custom-call | flops 2000000000 | bytes 3145728 | tf_op jit(solution)/shard_map/pallas_call | solution.py:304
  (110 shorter events, 47.2 us)
Async XLA Ops:
  12.2 31.2 %collective-permute-start.12 = (s16[1040,512]{1,0:T(8,128)(2,1)}, s16[1040,512]{1,0:T(8,128)(2,1)S(1)}, u32[]{:S(2)}, u32[]{:S(2)}) collective-permute-start(s16[1040,512]{1,0:T(8,128)(2,1)} %get-tuple-element.42), channel_id=1, source_target_pairs={{0,1},{1,2},{2,3},{3,0},{4,5},{5,6},{6,7},{7,4},{8,9},{9,10},{10,1... | collective-permute-start | bytes 3194888 | tf_op jit(solution)/shard_map/ppermute | solution.py:321
  14.7 34.0 %collective-permute-start.16 = (s16[1040,512]{1,0:T(8,128)(2,1)}, s16[1040,512]{1,0:T(8,128)(2,1)}, u32[]{:S(2)}, u32[]{:S(2)}) collective-permute-start(s16[1040,512]{1,0:T(8,128)(2,1)} %get-tuple-element.46), channel_id=1, source_target_pairs={{0,3},{1,0},{2,1},{3,2},{4,7},{5,4},{6,5},{7,6},{8,11},{9,8},{10,9... | collective-permute-start | bytes 3194888 | tf_op jit(solution)/shard_map/ppermute | solution.py:321
  24.6 35.8 %collective-permute-start.4 = (s16[1040,512]{1,0:T(8,128)(2,1)}, s16[1040,512]{1,0:T(8,128)(2,1)}, u32[]{:S(2)}, u32[]{:S(2)}) collective-permute-start(s16[1040,512]{1,0:T(8,128)(2,1)} %get-tuple-element.34), channel_id=1, source_target_pairs={{0,12},{1,13},{2,14},{3,15},{4,0},{5,1},{6,2},{7,3},{8,4},{9,5},{1... | collective-permute-start | bytes 3194888 | tf_op jit(solution)/shard_map/ppermute | solution.py:321
  27.1 36.0 %collective-permute-start = (s16[1040,512]{1,0:T(8,128)(2,1)}, s16[1040,512]{1,0:T(8,128)(2,1)}, u32[]{:S(2)}, u32[]{:S(2)}) collective-permute-start(s16[1040,512]{1,0:T(8,128)(2,1)} %get-tuple-element.30), channel_id=1, source_target_pairs={{0,4},{1,5},{2,6},{3,7},{4,8},{5,9},{6,10},{7,11},{8,12},{9,13},{1... | collective-permute-start | bytes 3194888 | tf_op jit(solution)/shard_map/ppermute | solution.py:321
  34.6 47.1 %collective-permute-start.14 = (s16[1040,512]{1,0:T(8,128)(2,1)}, s16[1040,512]{1,0:T(8,128)(2,1)S(1)}, u32[]{:S(2)}, u32[]{:S(2)}) collective-permute-start(s16[1040,512]{1,0:T(8,128)(2,1)} %get-tuple-element.43), channel_id=1, source_target_pairs={{0,3},{1,0},{2,1},{3,2},{4,7},{5,4},{6,5},{7,6},{8,11},{9,8},{10,9... | collective-permute-start | bytes 3194888 | tf_op jit(solution)/shard_map/ppermute | solution.py:321
  43.5 38.2 %collective-permute-start.15 = (s16[1040,512]{1,0:T(8,128)(2,1)}, s16[1040,512]{1,0:T(8,128)(2,1)S(1)}, u32[]{:S(2)}, u32[]{:S(2)}) collective-permute-start(s16[1040,512]{1,0:T(8,128)(2,1)} %get-tuple-element.44), channel_id=1, source_target_pairs={{0,1},{1,2},{2,3},{3,0},{4,5},{5,6},{6,7},{7,4},{8,9},{9,10},{10,1... | collective-permute-start | bytes 3194888 | tf_op jit(solution)/shard_map/ppermute | solution.py:321
  48.7 42.4 %collective-permute-start.13 = (s16[1040,512]{1,0:T(8,128)(2,1)}, s16[1040,512]{1,0:T(8,128)(2,1)S(1)}, u32[]{:S(2)}, u32[]{:S(2)}) collective-permute-start(s16[1040,512]{1,0:T(8,128)(2,1)} %shard_map.91), channel_id=1, source_target_pairs={{0,1},{1,2},{2,3},{3,0},{4,5},{5,6},{6,7},{7,4},{8,9},{9,10},{10,1... | collective-permute-start | bytes 3194888 | tf_op jit(solution)/shard_map/ppermute | solution.py:321
  60.4 43.9 %collective-permute-start.2 = (s16[1040,512]{1,0:T(8,128)(2,1)}, s16[1040,512]{1,0:T(8,128)(2,1)}, u32[]{:S(2)}, u32[]{:S(2)}) collective-permute-start(s16[1040,512]{1,0:T(8,128)(2,1)} %get-tuple-element.31), channel_id=1, source_target_pairs={{0,12},{1,13},{2,14},{3,15},{4,0},{5,1},{6,2},{7,3},{8,4},{9,5},{1... | collective-permute-start | bytes 3194888 | tf_op jit(solution)/shard_map/ppermute | solution.py:321
  63.0 35.8 %collective-permute-start.17 = (s16[1040,512]{1,0:T(8,128)(2,1)}, s16[1040,512]{1,0:T(8,128)(2,1)}, u32[]{:S(2)}, u32[]{:S(2)}) collective-permute-start(s16[1040,512]{1,0:T(8,128)(2,1)} %shard_map.93), channel_id=1, source_target_pairs={{0,3},{1,0},{2,1},{3,2},{4,7},{5,4},{6,5},{7,6},{8,11},{9,8},{10,9... | collective-permute-start | bytes 3194888 | tf_op jit(solution)/shard_map/ppermute | solution.py:321
  81.6 17.2 %copy-start = (s16[1040,512]{1,0:T(8,128)(2,1)}, s16[1040,512]{1,0:T(8,128)(2,1)S(1)}, u32[]{:S(2)}) copy-start(s16[1040,512]{1,0:T(8,128)(2,1)S(1)} %collective-permute-done.14.b0.refs_11_) | copy-start | bytes 3194884
  81.6 33.2 %collective-permute-start.3 = (s16[1040,512]{1,0:T(8,128)(2,1)}, s16[1040,512]{1,0:T(8,128)(2,1)}, u32[]{:S(2)}, u32[]{:S(2)}) collective-permute-start(s16[1040,512]{1,0:T(8,128)(2,1)} %get-tuple-element.32), channel_id=1, source_target_pairs={{0,4},{1,5},{2,6},{3,7},{4,8},{5,9},{6,10},{7,11},{8,12},{9,13},{1... | collective-permute-start | bytes 3194888 | tf_op jit(solution)/shard_map/ppermute | solution.py:321
  81.7 17.1 %copy-start.1 = (s16[1040,512]{1,0:T(8,128)(2,1)}, s16[1040,512]{1,0:T(8,128)(2,1)S(1)}, u32[]{:S(2)}) copy-start(s16[1040,512]{1,0:T(8,128)(2,1)S(1)} %collective-permute-done.15.a1.refs_12_) | copy-start | bytes 3194884
  81.7 35.8 %collective-permute-start.5 = (s16[1040,512]{1,0:T(8,128)(2,1)}, s16[1040,512]{1,0:T(8,128)(2,1)}, u32[]{:S(2)}, u32[]{:S(2)}) collective-permute-start(s16[1040,512]{1,0:T(8,128)(2,1)} %shard_map.82), channel_id=1, source_target_pairs={{0,12},{1,13},{2,14},{3,15},{4,0},{5,1},{6,2},{7,3},{8,4},{9,5},{1... | collective-permute-start | bytes 3194888 | tf_op jit(solution)/shard_map/ppermute | solution.py:321
  91.1 37.0 %collective-permute-start.1 = (s16[1040,512]{1,0:T(8,128)(2,1)}, s16[1040,512]{1,0:T(8,128)(2,1)}, u32[]{:S(2)}, u32[]{:S(2)}) collective-permute-start(s16[1040,512]{1,0:T(8,128)(2,1)} %shard_map.80), channel_id=1, source_target_pairs={{0,4},{1,5},{2,6},{3,7},{4,8},{5,9},{6,10},{7,11},{8,12},{9,13},{1... | collective-permute-start | bytes 3194888 | tf_op jit(solution)/shard_map/ppermute | solution.py:321
  101.7 36.7 %collective-permute-start.22 = (s16[1040,128]{1,0:T(8,128)(2,1)}, s16[1040,128]{1,0:T(8,128)(2,1)S(1)}, u32[]{:S(2)}, u32[]{:S(2)}) collective-permute-start(s16[1040,128]{1,0:T(8,128)(2,1)} %get-tuple-element.52), channel_id=1, source_target_pairs={{0,12},{1,13},{2,14},{3,15},{4,0},{5,1},{6,2},{7,3},{8,4},{9,5},{1... | collective-permute-start | bytes 798728 | tf_op jit(solution)/shard_map/ppermute | solution.py:321
  104.3 34.2 %collective-permute-start.18 = (s16[1040,128]{1,0:T(8,128)(2,1)}, s16[1040,128]{1,0:T(8,128)(2,1)S(1)}, u32[]{:S(2)}, u32[]{:S(2)}) collective-permute-start(s16[1040,128]{1,0:T(8,128)(2,1)} %get-tuple-element.48), channel_id=1, source_target_pairs={{0,4},{1,5},{2,6},{3,7},{4,8},{5,9},{6,10},{7,11},{8,12},{9,13},{1... | collective-permute-start | bytes 798728 | tf_op jit(solution)/shard_map/ppermute | solution.py:321
  114.8 41.3 %collective-permute-start.20 = (s16[1040,128]{1,0:T(8,128)(2,1)}, s16[1040,128]{1,0:T(8,128)(2,1)S(1)}, u32[]{:S(2)}, u32[]{:S(2)}) collective-permute-start(s16[1040,128]{1,0:T(8,128)(2,1)} %get-tuple-element.49), channel_id=1, source_target_pairs={{0,12},{1,13},{2,14},{3,15},{4,0},{5,1},{6,2},{7,3},{8,4},{9,5},{1... | collective-permute-start | bytes 798728 | tf_op jit(solution)/shard_map/ppermute | solution.py:321
  131.0 18.2 %collective-permute-start.10 = (s16[1040,128]{1,0:T(8,128)(2,1)}, s16[1040,128]{1,0:T(8,128)(2,1)}, u32[]{:S(2)}, u32[]{:S(2)}) collective-permute-start(s16[1040,128]{1,0:T(8,128)(2,1)} %get-tuple-element.40), channel_id=1, source_target_pairs={{0,3},{1,0},{2,1},{3,2},{4,7},{5,4},{6,5},{7,6},{8,11},{9,8},{10,9... | collective-permute-start | bytes 798728 | tf_op jit(solution)/shard_map/ppermute | solution.py:321
  131.3 20.1 %collective-permute-start.6 = (s16[1040,128]{1,0:T(8,128)(2,1)}, s16[1040,128]{1,0:T(8,128)(2,1)}, u32[]{:S(2)}, u32[]{:S(2)}) collective-permute-start(s16[1040,128]{1,0:T(8,128)(2,1)} %get-tuple-element.36), channel_id=1, source_target_pairs={{0,1},{1,2},{2,3},{3,0},{4,5},{5,6},{6,7},{7,4},{8,9},{9,10},{10,1... | collective-permute-start | bytes 798728 | tf_op jit(solution)/shard_map/ppermute | solution.py:321
  138.4 17.8 %collective-permute-start.21 = (s16[1040,128]{1,0:T(8,128)(2,1)}, s16[1040,128]{1,0:T(8,128)(2,1)S(1)}, u32[]{:S(2)}, u32[]{:S(2)}) collective-permute-start(s16[1040,128]{1,0:T(8,128)(2,1)} %get-tuple-element.50), channel_id=1, source_target_pairs={{0,4},{1,5},{2,6},{3,7},{4,8},{5,9},{6,10},{7,11},{8,12},{9,13},{1... | collective-permute-start | bytes 798728 | tf_op jit(solution)/shard_map/ppermute | solution.py:321
  138.4 20.5 %collective-permute-start.8 = (s16[1040,128]{1,0:T(8,128)(2,1)}, s16[1040,128]{1,0:T(8,128)(2,1)S(1)}, u32[]{:S(2)}, u32[]{:S(2)}) collective-permute-start(s16[1040,128]{1,0:T(8,128)(2,1)} %get-tuple-element.37), channel_id=1, source_target_pairs={{0,3},{1,0},{2,1},{3,2},{4,7},{5,4},{6,5},{7,6},{8,11},{9,8},{10,9... | collective-permute-start | bytes 798728 | tf_op jit(solution)/shard_map/ppermute | solution.py:321
  149.2 11.3 %collective-permute-start.9 = (s16[1040,128]{1,0:T(8,128)(2,1)S(1)}, s16[1040,128]{1,0:T(8,128)(2,1)S(1)}, u32[]{:S(2)}, u32[]{:S(2)}) collective-permute-start(s16[1040,128]{1,0:T(8,128)(2,1)S(1)} %copy-done.20), channel_id=1, source_target_pairs={{0,1},{1,2},{2,3},{3,0},{4,5},{5,6},{6,7},{7,4},{8,9},{9,10},{10,1... | collective-permute-start | bytes 798728 | tf_op jit(solution)/shard_map/ppermute | solution.py:321
  151.4 9.1 %collective-permute-start.23 = (s16[1040,128]{1,0:T(8,128)(2,1)S(1)}, s16[1040,128]{1,0:T(8,128)(2,1)S(1)}, u32[]{:S(2)}, u32[]{:S(2)}) collective-permute-start(s16[1040,128]{1,0:T(8,128)(2,1)S(1)} %copy-done.14), channel_id=1, source_target_pairs={{0,12},{1,13},{2,14},{3,15},{4,0},{5,1},{6,2},{7,3},{8,4},{9,5},{1... | collective-permute-start | bytes 798728 | tf_op jit(solution)/shard_map/ppermute | solution.py:321
  156.1 6.8 %collective-permute-start.19 = (s16[1040,128]{1,0:T(8,128)(2,1)S(1)}, s16[1040,128]{1,0:T(8,128)(2,1)S(1)}, u32[]{:S(2)}, u32[]{:S(2)}) collective-permute-start(s16[1040,128]{1,0:T(8,128)(2,1)S(1)} %copy-done.15), channel_id=1, source_target_pairs={{0,4},{1,5},{2,6},{3,7},{4,8},{5,9},{6,10},{7,11},{8,12},{9,13},{1... | collective-permute-start | bytes 798728 | tf_op jit(solution)/shard_map/ppermute | solution.py:321
  156.2 6.7 %collective-permute-start.11 = (s16[1040,128]{1,0:T(8,128)(2,1)}, s16[1040,128]{1,0:T(8,128)(2,1)S(1)}, u32[]{:S(2)}, u32[]{:S(2)}) collective-permute-start(s16[1040,128]{1,0:T(8,128)(2,1)} %shard_map.87), channel_id=1, source_target_pairs={{0,3},{1,0},{2,1},{3,2},{4,7},{5,4},{6,5},{7,6},{8,11},{9,8},{10,9... | collective-permute-start | bytes 798728 | tf_op jit(solution)/shard_map/ppermute | solution.py:321
  158.9 8.0 %collective-permute-start.7 = (s16[1040,128]{1,0:T(8,128)(2,1)}, s16[1040,128]{1,0:T(8,128)(2,1)S(1)}, u32[]{:S(2)}, u32[]{:S(2)}) collective-permute-start(s16[1040,128]{1,0:T(8,128)(2,1)} %shard_map.85), channel_id=1, source_target_pairs={{0,1},{1,2},{2,3},{3,0},{4,5},{5,6},{6,7},{7,4},{8,9},{9,10},{10,1... | collective-permute-start | bytes 798728 | tf_op jit(solution)/shard_map/ppermute | solution.py:321
  178.9 22.1 %copy-start.18 = (f32[32,256]{1,0:T(8,128)}, f32[32,256]{1,0:T(8,128)S(1)}, u32[]{:S(2)}) copy-start(f32[32,256]{1,0:T(8,128)S(1)} %pad_maximum_fusion.1.refs_0_) | copy-start | bytes 98308
  178.9 9.6 %collective-permute-start.24 = (f32[32,256]{1,0:T(8,128)S(1)}, f32[32,256]{1,0:T(8,128)S(1)}, u32[]{:S(2)}, u32[]{:S(2)}) collective-permute-start(f32[32,256]{1,0:T(8,128)S(1)} %pad_maximum_fusion.1.refs_0_), channel_id=1, source_target_pairs={{0,16},{16,0},{32,48},{48,32},{64,80},{80,64},{96,112},{112,96},{1... | collective-permute-start | bytes 98312 | tf_op jit(solution)/shard_map/ppermute | solution.py:358
  188.6 12.4 %copy-start.19 = (f32[32,256]{1,0:T(8,128)}, f32[32,256]{1,0:T(8,128)S(1)}, u32[]{:S(2)}) copy-start(f32[32,256]{1,0:T(8,128)S(1)} %collective-permute-done.24.refs_1_) | copy-start | bytes 98308
  189.3 12.7 %collective-permute-start.27 = (f32[64,256]{1,0:T(8,128)S(1)}, f32[64,256]{1,0:T(8,128)S(1)}, u32[]{:S(2)}, u32[]{:S(2)}) collective-permute-start(f32[64,256]{1,0:T(8,128)S(1)} %pad_maximum_fusion), channel_id=1, source_target_pairs={{0,96},{16,112},{32,0},{48,16},{64,32},{80,48},{96,64},{112,80},{1... | collective-permute-start | bytes 196616 | tf_op jit(solution)/shard_map/ppermute | solution.py:362
  201.0 4.7 %collective-permute-start.26 = (f32[64,256]{1,0:T(8,128)S(1)}, f32[64,256]{1,0:T(8,128)S(1)}, u32[]{:S(2)}, u32[]{:S(2)}) collective-permute-start(f32[64,256]{1,0:T(8,128)S(1)} %pad_maximum_fusion), channel_id=1, source_target_pairs={{0,64},{16,80},{32,96},{48,112},{64,0},{80,16},{96,32},{112,48},{1... | collective-permute-start | bytes 196616 | tf_op jit(solution)/shard_map/ppermute | solution.py:362
  201.4 6.0 %collective-permute-start.25 = (f32[64,256]{1,0:T(8,128)S(1)}, f32[64,256]{1,0:T(8,128)S(1)}, u32[]{:S(2)}, u32[]{:S(2)}) collective-permute-start(f32[64,256]{1,0:T(8,128)S(1)} %pad_maximum_fusion), channel_id=1, source_target_pairs={{0,32},{16,48},{32,64},{48,80},{64,96},{80,112},{96,0},{112,16},{1... | collective-permute-start | bytes 196616 | tf_op jit(solution)/shard_map/ppermute | solution.py:362
  (17 other events, 69.7 us)
